TPU v7x, 32 devices: a whole 2x2x4 slice. The times are simulated.
32 devices in a mesh: lr: 8 (over y, x, core), lc: 4 (over z).
Axes of the slice: x: 2, y: 2, z: 4, core: 2. Of those that a mesh axis runs over, the one named last changes fastest.
Arguments:
- queries: bfloat16 [2048, 768], P(('lr', 'lc')), may hold values from -6 to 6
- probes: int32 [2048, 16], P(('lr', 'lc')), may hold values from 0 to 255, as said below
- assign: int32 [2048], P(('lr', 'lc')), may hold values from 0 to 255, as said below
- list_rows: bfloat16 [256, 1024, 768], P(('lr', 'lc')), may hold values from -0.21875 to 0.21875
- list_fill: int32 [256], P(('lr', 'lc')), may hold values from 1 to 1024
- centroids: float32 [256, 768], P(('lr', 'lc')), may hold values from -6 to 6
- list_sums: float32 [256, 768], P(('lr', 'lc')), may hold values from -6 to 6
Outputs:
- dup_max: float32 [2048, 16], P(('lr', 'lc'))
- codes: bfloat16 [256, 16, 768], P(('lr', 'lc'))
- scales: float32 [256, 16], P(('lr', 'lc'))
- new_sums: float32 [256, 768], P(('lr', 'lc'))
Inputs may be any that keep to these rules, and one draw needn't show every extreme that they name: A list id is 8 times its owner's device index along lr+lc plus its place there. The probe pairs of one device's new vectors name lists of one owner at most 64 times, and one list is named by at most 256 pairs over all new vectors; both bounds are reached. A vector's probes may repeat a list. `assign`: one device's new vectors go to lists of one owner at most 4 times, and one list receives at most 16 new vectors; both bounds are reached.
All inputs are finite; a program needn't handle non-finite values. Where the computation divides by a largest or mean magnitude, that divisor is 1e-20 or more.
Results may differ from a plain program's by a relative error of at most 0.001.
Values may be sent and summed in bfloat16 or wider, within the bound.
No kernel may reach another device: no remote copies, remote signals or barrier semaphores. Data moves between devices by JAX's collectives and lax.ppermute only.
A program may use at most 64 MiB of HBM per device.

v0:
```python
import functools

import jax
import jax.numpy as jnp
from jax import lax
from jax.experimental import pallas as pl
from jax.experimental.pallas import tpu as pltpu
from jax.sharding import PartitionSpec as P

AXES = ("lr", "lc")
VMEM = pl.BlockSpec(memory_space=pltpu.VMEM)
SMEM = pl.BlockSpec(memory_space=pltpu.SMEM)
BF16 = jnp.bfloat16
F32 = jnp.float32
LISTS_A_STEP = 4


def call(body, out_shape, *args, specs, name, scratch=(), flops=0, limit=24, alias=None):
    many = isinstance(out_shape, (list, tuple))
    return pl.pallas_call(
        body,
        in_specs=list(specs),
        out_specs=[VMEM] * len(out_shape) if many else VMEM,
        out_shape=out_shape,
        scratch_shapes=list(scratch),
        input_output_aliases=alias or {},
        compiler_params=pltpu.CompilerParams(vmem_limit_bytes=limit * 2**20),
        cost_estimate=pl.CostEstimate(flops=flops, bytes_accessed=0, transcendentals=0),
        name=name,
    )(*args)


def iota(shape, dim):
    return lax.broadcasted_iota(jnp.int32, shape, dim)


def over(x, n):
    if n & (n - 1):
        return x // n, x % n
    return x >> (n.bit_length() - 1), x & (n - 1)


def unpack(q_refs, src_ref, first, list_count, id_rows, dim, marks_ref):
    half = marks_ref.shape[1] // 2
    me = src_ref[src_ref.shape[0] - 1]
    marks_ref[...] = jnp.zeros(marks_ref.shape, F32)
    lists = iota((list_count, 2 * half), 0)
    lane = iota((list_count, 2 * half), 1)
    for q_ref in q_refs:
        for p in range(q_ref.shape[0] // (2 * half)):
            ids = q_ref[p * 2 * half : (p + 1) * 2 * half, dim:].astype(F32).T
            owners, places = ids[:id_rows], ids[ids.shape[0] // 2 : ids.shape[0] // 2 + id_rows]
            places = jnp.where(owners == me.astype(F32), places, -1.0).astype(jnp.int32)
            probed = jnp.zeros(lists.shape, jnp.int32)
            for l in range(list_count):
                hit = jnp.where(places[: id_rows - 1] == l, 1, 0)
                probed = jnp.where(lists == l, jnp.max(hit, axis=0, keepdims=True), probed)
            probed = probed.astype(F32)
            appended = jnp.where(places[id_rows - 1 :] == lists, 1.0, 0.0)
            turned = [pltpu.roll(x, half, 1) for x in (probed, appended)]
            for i, block in enumerate(
                (jnp.where(lane < half, probed, turned[1]), jnp.where(lane < half, turned[0], appended))
            ):
                start = pl.multiple_of(src_ref[first] * list_count, list_count)
                marks_ref[pl.ds(start, list_count), :] = block
                first += 1


def rank_marks(list_count, marks, past=None):
    rows, width = marks.shape
    half = width // 2
    a, b = iota((width, width), 0), iota((width, width), 1)
    same = over(a, half)[0] == over(b, half)[0]
    earlier = jnp.where(same & (a < b), 1.0, 0.0).astype(BF16)
    every = jnp.where(same, 1.0, 0.0).astype(BF16)
    r, s = iota((rows, rows), 0), iota((rows, rows), 1)
    alike = over(r, list_count)[1] == over(s, list_count)[1]
    before = jnp.where(alike & (s < r), 1.0, 0.0).astype(BF16)

    def counts(x):
        return jnp.dot(x.astype(BF16), every, preferred_element_type=F32).astype(BF16)

    place = jnp.dot(marks.astype(BF16), earlier, preferred_element_type=F32)
    place = place + jnp.dot(before, counts(marks), preferred_element_type=F32)
    if past is not None:
        place = place + jnp.dot(
            jnp.where(alike, 1.0, 0.0).astype(BF16), counts(past), preferred_element_type=F32
        )
    return jnp.where(marks > 0.5, place, -1.0).astype(jnp.int32)


def pair_ranks(ranks_ref, src_ref, first, list_count, half, part):
    blocks = []
    for i in range(2):
        start = pl.multiple_of(src_ref[first + i] * list_count, list_count)
        block = ranks_ref[pl.ds(start, list_count), :]
        blocks.append(block if i == part else pltpu.roll(block, half, 1))
    lane = iota(blocks[0].shape, 1)
    return jnp.where(lane < half, blocks[0], blocks[1])


def group_into(list_count, per_list, first_piece, src_ref, ranks_ref, old, q_refs, out_ref, pick, pairs_ref, starts):
    half = ranks_ref.shape[1] // 2
    depth = pick.shape[1]
    dim = out_ref.shape[1]
    lists_a_step = LISTS_A_STEP
    block = pick.shape[0] // lists_a_step
    pair_count = depth // (2 * half)
    lowest = highest = None
    for p in range(pair_count):
        ranks = pair_ranks(ranks_ref, src_ref, first_piece + 2 * p, list_count, half, 0)
        pairs_ref[p * list_count : (p + 1) * list_count, :] = ranks
        low = jnp.where(ranks < 0, per_list, ranks)
        lowest = low if p == 0 else jnp.minimum(lowest, low)
        highest = ranks if p == 0 else jnp.maximum(highest, ranks)
    low = jnp.min(lowest, axis=1, keepdims=True)
    low = jnp.minimum(low - (low & 15), per_list - block) if old else jnp.zeros_like(low)
    high = jnp.max(highest, axis=1, keepdims=True)
    beyond = sum((high >= low + k * block).astype(jnp.int32) for k in range(1, -(-per_list // block)))
    firsts = []
    for l in range(list_count):
        firsts.append(low[l, 0] if old else 0)
        starts[l] = firsts[l]
        starts[list_count + l] = beyond[l, 0]
    place = iota((block, 2 * half), 0).astype(BF16)
    one, none = jnp.ones(place.shape, BF16), jnp.zeros(place.shape, BF16)

    def product(count):
        total = None
        at = 0
        for q_ref in q_refs:
            n = q_ref.shape[0]
            term = jnp.dot(pick[:count, at : at + n], q_ref[:, :dim], preferred_element_type=F32)
            total = term if total is None else total + term
            at += n
        return total.astype(BF16)

    for step in range(list_count // lists_a_step):
        for i in range(lists_a_step):
            l = step * lists_a_step + i
            for p in range(pair_count):
                ranks = pairs_ref[p * list_count + l : p * list_count + l + 1, :] - firsts[l]
                pick[i * block : (i + 1) * block, p * 2 * half : (p + 1) * 2 * half] = jnp.where(
                    ranks.astype(F32).astype(BF16) == place, one, none
                )
        total = product(pick.shape[0])
        for i in range(lists_a_step):
            l = step * lists_a_step + i
            rows = pl.ds(pl.multiple_of(l * per_list + firsts[l], 16), block)
            part = total[i * block : (i + 1) * block]
            out_ref[rows, :] = out_ref[rows, :] + part if old else part
            if not old:
                out_ref[l * per_list + block : (l + 1) * per_list, :] = jnp.zeros((per_list - block, dim), BF16)

    @pl.loop(0, list_count)
    def _(l):
        @pl.loop(1, starts[list_count + l] + 1)
        def _(k):
            low = starts[l] + k * block
            first = jnp.minimum(low, per_list - block)
            for p in range(pair_count):
                ranks = pairs_ref[pl.ds(p * list_count + l, 1), :]
                ranks = jnp.where(ranks >= low, ranks - first, -1)
                pick[:block, p * 2 * half : (p + 1) * 2 * half] = jnp.where(
                    ranks.astype(F32).astype(BF16) == place, one, none
                )
            rows = pl.ds(pl.multiple_of(l * per_list + first, 16), block)
            out_ref[rows, :] = out_ref[rows, :] + product(block)


def group_body(list_count, per_list, id_rows, first_piece, src_ref, *refs):
    old, q_refs = (refs[:3], refs[3:-6]) if first_piece else (None, refs[:-6])
    out_ref, marks_ref, ranks_ref, pick, pairs, starts = refs[-6:]
    unpack(q_refs, src_ref, first_piece, list_count, id_rows, out_ref.shape[1], marks_ref)
    ranks_ref[...] = rank_marks(list_count, marks_ref[...], old[1][...] if old else None)
    group_into(
        list_count, per_list, first_piece, src_ref, ranks_ref, bool(old), q_refs, out_ref, pick, pairs, starts
    )
    if old:
        marks_ref[...] = marks_ref[...] + old[1][...]
        ranks_ref[...] = jnp.maximum(ranks_ref[...], old[2][...])


def score_body(per_list, id_rows, first_piece, fill_ref, rows, src_ref, old_marks_ref, old_ranks_ref, _, *refs):
    q_refs, (out_ref, marks_ref, grouped_ref, ranks_ref, pick, best, pairs, starts) = refs[:-8], refs[-8:]
    list_count, _, dim = rows.shape
    width = out_ref.shape[1]
    senders = ranks_ref.shape[0] // list_count
    unpack(q_refs, src_ref, first_piece, list_count, id_rows, dim, marks_ref)
    ranks_ref[...] = rank_marks(list_count, marks_ref[...], old_marks_ref[...])
    group_into(list_count, per_list, first_piece, src_ref, ranks_ref, True, q_refs, grouped_ref, pick, pairs, starts)
    for l in range(list_count):
        scores = lax.dot_general(
            rows[l],
            grouped_ref[l * per_list : (l + 1) * per_list, :],
            (((1,), (1,)), ((), ())),
            preferred_element_type=F32,
        )
        scores = jnp.where(iota(scores.shape, 0) < fill_ref[l], scores, -jnp.inf)
        best[l : l + 1, :] = jnp.max(scores, axis=0, keepdims=True)
    for s in range(senders):
        at = slice(s * list_count, (s + 1) * list_count)
        ranks = jnp.maximum(ranks_ref[at, :], old_ranks_ref[at, :])
        found = jnp.zeros(ranks.shape, F32)
        for c in range(per_list // width):
            index = jnp.clip(ranks - c * width, 0, width - 1)
            got = jnp.take_along_axis(best[:, c * width : (c + 1) * width], index, axis=1)
            found = jnp.where((ranks >= c * width) & (ranks < (c + 1) * width), got, found)
        lane = iota((list_count // 2, width), 1)
        turned = pltpu.roll(found, width // 2, 1)
        packed = jnp.where(lane < width // 2, found[: list_count // 2], turned[list_count // 2 :])
        out_ref[s * (list_count // 2) : (s + 1) * (list_count // 2), :] = packed


def pick_body(list_count, got_ref, ids_ref, out_ref):
    probe_count, count = ids_ref.shape
    half = list_count // 2
    owner, place = over(ids_ref[...], list_count)
    second = jnp.where(place >= half, 1, 0)
    row = owner * half + place - second * half
    rows = iota(got_ref.shape, 0)
    row = jnp.concatenate([jnp.where(second == 0, row, -1), jnp.where(second == 1, row, -1)], axis=1)
    got = got_ref[...]
    found = []
    for j in range(probe_count):
        found.append(jnp.sum(jnp.where(rows == row[j : j + 1, :], got, 0.0), axis=0, keepdims=True))
    found = jnp.concatenate(found, axis=0)
    out_ref[...] = found[:, :count] + found[:, count:]


def append_body(list_count, slots, src_ref, old_marks_ref, marks_ref, center_ref, sums_ref, *refs):
    q_refs, (codes_ref, scales_ref, sums_out_ref, ranks_ref, pick) = refs[:-5], refs[-5:]
    ranks_ref[...] = rank_marks(list_count, old_marks_ref[...] + marks_ref[...])
    half = ranks_ref.shape[1] // 2
    dim = center_ref.shape[1]
    place = iota((slots, 2 * half), 0)
    piece = 0
    total = jnp.zeros((list_count * slots, dim), F32)
    live = jnp.zeros((list_count * slots, 1), F32)
    for q_ref in q_refs:
        n = q_ref.shape[0]
        for p in range(n // (2 * half)):
            ranks = pair_ranks(ranks_ref, src_ref, piece, list_count, half, 1)
            piece += 2
            for l in range(list_count):
                hit = jnp.where(ranks[l : l + 1, :] == place, 1.0, 0.0)
                pick[l * slots : (l + 1) * slots, p * 2 * half : (p + 1) * 2 * half] = hit.astype(BF16)
        chosen = pick[:, :n]
        live = live + jnp.sum(chosen.astype(F32), axis=1, keepdims=True)
        total = total + jnp.dot(chosen, q_ref[:, :dim], preferred_element_type=F32)
    for l in range(list_count):
        rows = slice(l * slots, (l + 1) * slots)
        used = live[rows, :] > 0.5
        residual = jnp.where(used, total[rows, :] - center_ref[l : l + 1, :], 0.0)
        scale = jnp.max(jnp.abs(residual), axis=1, keepdims=True) + 1e-6
        codes_ref[l] = (residual / scale).astype(BF16)
        scales_ref[l : l + 1, :] = jnp.where(used, scale, 0.0).T
        sums_out_ref[l : l + 1, :] = sums_ref[l : l + 1, :] + jnp.sum(residual, axis=0, keepdims=True)


def swap_pairs(rows, cols, of):
    pairs = []
    for lr in range(rows):
        for lc in range(cols):
            to = of(lr, lc)
            pairs.append((lr * cols + lc, to[0] * cols + to[1]))
    return pairs


def after(x, *others):
    return lax.optimization_barrier((x, *others))[0]


def swap_core(x, rows, cols):
    return lax.ppermute(x, AXES, swap_pairs(rows, cols, lambda r, c: (r ^ 1, c)))


def gather_queries(queries, rows, cols, group_early):
    me = lax.axis_index(AXES)
    if (rows, cols) != (8, 4):
        whole = lax.all_gather(queries, AXES, axis=0, tiled=True)
        half = whole.shape[0] // 2
        sources = jnp.append(jnp.arange(rows * cols, dtype=jnp.int32), me)
        return [whole[:half]], [whole[half:]], sources, group_early(sources, [whole[:half]])

    def send(x, of):
        return lax.ppermute(x, AXES, swap_pairs(rows, cols, of))

    def first(x):
        return jnp.concatenate([x, send(x, lambda r, c: (r ^ (4 if r & 1 else 2), c))], 0)

    def second(x):
        return jnp.concatenate([x, send(x, lambda r, c: (r ^ (2 if r & 1 else 4), c))], 0)

    def other(x):
        return [x, swap_core(x, rows, cols)]

    r, c = lax.axis_index("lr"), lax.axis_index("lc")
    sources = []
    for planes in ((0, 1), (2, 3)):
        for core in (0, 1):
            odd = (r ^ core) & 1
            one, two = jnp.where(odd == 1, 4, 2), jnp.where(odd == 1, 2, 4)
            for hops in range(4):
                row = r ^ core
                row = row ^ one if hops & 1 else row
                row = row ^ two if hops & 2 else row
                sources += [row * cols + (c ^ plane) for plane in planes]
    sources = jnp.stack(sources + [me]).astype(jnp.int32)

    z1, z2, z3 = (send(queries, lambda r, c, k=k: (r, c ^ k)) for k in (1, 2, 3))
    pair = jnp.concatenate([queries, z1], 0)
    far = jnp.concatenate([z2, z3], 0)
    near = second(first(pair))
    far = second(first(far))
    pieces = near.shape[0] // queries.shape[0]
    half = group_early(sources, [near])
    part = other(after(near, *half))
    part[0] = near
    grouped = group_early(sources, part[1:], pieces, tuple(half))
    return part, other(far), sources, grouped


def local(queries, probes, assign, list_rows, list_fill, centroids, list_sums):
    rows, cols = lax.axis_size("lr"), lax.axis_size("lc")
    group = rows * cols
    list_count, row_count, dim = list_rows.shape
    query_count, probe_count = probes.shape
    pair_cap = 2 * query_count * probe_count // group
    append_cap = max(2, 2 * query_count // group)
    per_list = group * pair_cap // list_count
    slots = group * append_cap // list_count
    width = 2 * query_count
    total_lists = group * list_count

    ids = jnp.concatenate([probes, assign[:, None]], axis=1)
    id_rows = probe_count + 1
    id_lanes = 64
    spare = jnp.zeros((query_count, id_lanes - id_rows), jnp.int32)
    digits = jnp.concatenate([ids // list_count, spare, ids % list_count, spare], axis=1)
    packed = jnp.concatenate([queries, digits.astype(BF16)], axis=1)

    marks_shape = jax.ShapeDtypeStruct((total_lists, width), F32)
    ranks_shape = jax.ShapeDtypeStruct((total_lists, width), jnp.int32)

    def working(depth):
        share = -(-per_list * depth // (group * query_count * 16)) * 16
        return [
            pltpu.VMEM((LISTS_A_STEP * min(per_list, share + 16), depth), BF16),
            pltpu.VMEM((depth // width * list_count, width), jnp.int32),
            pltpu.SMEM((2 * list_count,), jnp.int32),
        ]

    def group_early(sources, part, first=0, old=()):
        depth = sum(x.shape[0] for x in part)
        return call(
            functools.partial(group_body, list_count, per_list, id_rows, first),
            [jax.ShapeDtypeStruct((list_count * per_list, dim), BF16), marks_shape, ranks_shape],
            sources,
            *old,
            *part,
            specs=[SMEM] + [VMEM] * (len(old) + len(part)),
            scratch=working(depth),
            flops=2 * list_count * per_list * depth * dim,
            limit=28,
            alias={1: 0} if old else None,
            name="group",
        )

    part, rest, sources, (grouped, old_marks, old_ranks) = gather_queries(packed, rows, cols, group_early)
    chunks = part + rest
    first = sum(x.shape[0] for x in part) // query_count
    depth = sum(x.shape[0] for x in rest)
    best, marks, _ = call(
        functools.partial(score_body, per_list, id_rows, first),
        [
            jax.ShapeDtypeStruct((total_lists // 2, width), F32),
            marks_shape,
            jax.ShapeDtypeStruct(grouped.shape, BF16),
        ],
        list_fill,
        list_rows,
        sources,
        old_marks,
        old_ranks,
        grouped,
        *rest,
        specs=[SMEM, VMEM, SMEM] + [VMEM] * (3 + len(rest)),
        scratch=[
            pltpu.VMEM((total_lists, width), jnp.int32),
            working(depth)[0],
            pltpu.VMEM((list_count, per_list), F32),
            *working(depth)[1:],
        ],
        alias={5: 2},
        limit=28,
        name="score",
    )
    got = lax.all_to_all(
        best.reshape(group, list_count // 2, width), AXES, split_axis=0, concat_axis=0, tiled=True
    )
    dup_max = call(
        functools.partial(pick_body, list_count),
        jax.ShapeDtypeStruct((probe_count, query_count), F32),
        got.reshape(total_lists // 2, width),
        probes.T,
        specs=[VMEM, VMEM],
        name="pick",
    )

    codes, scales, new_sums = call(
        functools.partial(append_body, list_count, slots),
        [
            jax.ShapeDtypeStruct((list_count, slots, dim), BF16),
            jax.ShapeDtypeStruct((list_count, slots), F32),
            jax.ShapeDtypeStruct((list_count, dim), F32),
        ],
        sources,
        old_marks,
        marks,
        centroids,
        list_sums,
        *chunks,
        specs=[SMEM] + [VMEM] * (4 + len(chunks)),
        scratch=[pltpu.VMEM((total_lists, width), jnp.int32), pltpu.VMEM((list_count * slots, max(x.shape[0] for x in chunks)), BF16)],
        name="append",
    )
    return dup_max.T, codes, scales, new_sums


def solution(mesh):
    split = P(AXES, None)
    return jax.shard_map(
        local,
        mesh=mesh,
        in_specs=(split, split, P(AXES), P(AXES, None, None), P(AXES), split, split),
        out_specs=(split, P(AXES, None, None), split, split),
        check_vma=False,
    )
```

profile of v0, /device:TPU:0, one launch (start us, length us, event | category | flops | bytes accessed | tf_op | source)
XLA Modules:
  0.0 59.3 jit_solution(11150907626035098453)
XLA Ops:
  0.6 0.7 %pad_add_fusion = s32[64,17]{0,1:T(8,128)S(1)} fusion(s32[64,1]{0,1:T(1,128)} %bitcast.40, s32[64,16]{0,1:T(8,128)} %param.8), kind=kLoop, calls=%fused_computation.15 | loop fusion | flops 1088 | bytes 8704 | tf_op jit(solution)/shard_map/concatenate | solution.py:336
  1.4 0.1 copy.15
  1.5 1.0 %concatenate.32 = bf16[64,896]{1,0:T(8,128)(2,1)S(1)} concatenate(bf16[64,768]{1,0:T(8,128)(2,1)} %param.7, bf16[64,17]{1,0:T(8,128)(2,1)S(1)} %get-tuple-element.29, bf16[64,47]{1,0:T(8,128)(2,1)S(1)} %broadcast_in_dim.7, bf16[64,17]{1,0:T(8,128)(2,1)S(1)} %get-tuple-element.28, bf16[64,47]{1,0:T(8,128)(2,1)S(1)} %broadcast_in_dim.7), dimensions={1} | concatenate | bytes 229376 | tf_op jit(solution)/shard_map/concatenate | solution.py:341
  2.5 3.1 %collective-permute-start = (bf16[64,896]{1,0:T(8,128)(2,1)S(1)}, bf16[64,896]{1,0:T(8,128)(2,1)S(1)}, u32[]{:S(2)}, u32[]{:S(2)}) collective-permute-start(bf16[64,896]{1,0:T(8,128)(2,1)S(1)} %concatenate.32), channel_id=1, source_target_pairs={{0,1},{1,0},{2,3},{3,2},{4,5},{5,4},{6,7},{7,6},{8,9},{9,8},{10,11... | collective-permute-start | bytes 344072 | tf_op jit(solution)/shard_map/ppermute | solution.py:287
  5.6 2.6 %collective-permute-start.4 = (bf16[64,896]{1,0:T(8,128)(2,1)S(1)}, bf16[64,896]{1,0:T(8,128)(2,1)S(1)}, u32[]{:S(2)}, u32[]{:S(2)}) collective-permute-start(bf16[64,896]{1,0:T(8,128)(2,1)S(1)} %concatenate.32), channel_id=1, source_target_pairs={{0,2},{1,3},{2,0},{3,1},{4,6},{5,7},{6,4},{7,5},{8,10},{9,11},{10,... | collective-permute-start | bytes 344072 | tf_op jit(solution)/shard_map/ppermute | solution.py:287
  8.2 0.6 collective-permute-done
  8.8 2.9 %collective-permute-start.1 = (bf16[128,896]{1,0:T(8,128)(2,1)S(1)}, bf16[128,896]{1,0:T(8,128)(2,1)S(1)}, u32[]{:S(2)}, u32[]{:S(2)}) collective-permute-start(bf16[128,896]{1,0:T(8,128)(2,1)S(1)} %pad_maximum_fusion.3), channel_id=1, source_target_pairs={{0,8},{1,9},{2,10},{3,11},{4,20},{5,21},{6,22},{7,23},{8,0},{9,1},... | collective-permute-start | bytes 688136 | tf_op jit(solution)/shard_map/ppermute | solution.py:287
  11.7 5.6 %collective-permute-done.4 = bf16[64,896]{1,0:T(8,128)(2,1)S(1)} collective-permute-done((bf16[64,896]{1,0:T(8,128)(2,1)S(1)}, bf16[64,896]{1,0:T(8,128)(2,1)S(1)}, u32[]{:S(2)}, u32[]{:S(2)}) %collective-permute-start.4) | collective-permute-done | bytes 114720 | tf_op jit(solution)/shard_map/ppermute | solution.py:287
  17.3 1.6 %collective-permute-start.6 = (bf16[128,896]{1,0:T(8,128)(2,1)S(1)}, bf16[128,896]{1,0:T(8,128)(2,1)S(1)}, u32[]{:S(2)}, u32[]{:S(2)}) collective-permute-start(bf16[128,896]{1,0:T(8,128)(2,1)S(1)} %pad_maximum_fusion.4), channel_id=1, source_target_pairs={{0,8},{1,9},{2,10},{3,11},{4,20},{5,21},{6,22},{7,23},{8,0},{9,1},... | collective-permute-start | bytes 688136 | tf_op jit(solution)/shard_map/ppermute | solution.py:287
  18.9 0.0 collective-permute-done.1
  18.9 1.6 %collective-permute-start.2 = (bf16[256,896]{1,0:T(8,128)(2,1)S(1)}, bf16[256,896]{1,0:T(8,128)(2,1)S(1)}, u32[]{:S(2)}, u32[]{:S(2)}) collective-permute-start(bf16[256,896]{1,0:T(8,128)(2,1)S(1)} %pad_maximum_fusion.1), channel_id=1, source_target_pairs={{0,16},{1,17},{2,18},{3,19},{4,12},{5,13},{6,14},{7,15},{8,24},{9,... | collective-permute-start | bytes 1376264 | tf_op jit(solution)/shard_map/ppermute | solution.py:287
  20.5 0.1 stack.132.src_ref
  20.6 5.3 %collective-permute-done.6 = bf16[128,896]{1,0:T(8,128)(2,1)S(1)} collective-permute-done((bf16[128,896]{1,0:T(8,128)(2,1)S(1)}, bf16[128,896]{1,0:T(8,128)(2,1)S(1)}, u32[]{:S(2)}, u32[]{:S(2)}) %collective-permute-start.6) | collective-permute-done | bytes 229408 | tf_op jit(solution)/shard_map/ppermute | solution.py:287
  25.9 1.6 %collective-permute-start.7 = (bf16[256,896]{1,0:T(8,128)(2,1)S(1)}, bf16[256,896]{1,0:T(8,128)(2,1)S(1)}, u32[]{:S(2)}, u32[]{:S(2)}) collective-permute-start(bf16[256,896]{1,0:T(8,128)(2,1)S(1)} %pad_maximum_fusion.2), channel_id=1, source_target_pairs={{0,16},{1,17},{2,18},{3,19},{4,12},{5,13},{6,14},{7,15},{8,24},{9,... | collective-permute-start | bytes 1376264 | tf_op jit(solution)/shard_map/ppermute | solution.py:287
  27.6 0.0 collective-permute-done.2
  27.6 0.1 pad_maximum_fusion.refs_0_
  27.7 0.0 copy-start
  27.7 2.1 %group.2 = (bf16[2048,768]{1,0:T(8,128)(2,1)S(1)}, f32[256,128]{1,0:T(8,128)S(1)}, s32[256,128]{1,0:T(8,128)S(1)}) custom-call(s32[33]{0:T(128)S(1)} %stack.132.src_ref, bf16[512,896]{1,0:T(8,128)(2,1)S(1)} %pad_maximum_fusion.refs_0_), custom_call_target="tpu_custom_call" | custom-call | flops 1610612736 | tf_op jit(solution)/shard_map/group/pallas_call | solution.py:20
  29.7 0.1 collective-permute-start.3
  29.9 4.6 %collective-permute-done.7 = bf16[256,896]{1,0:T(8,128)(2,1)S(1)} collective-permute-done((bf16[256,896]{1,0:T(8,128)(2,1)S(1)}, bf16[256,896]{1,0:T(8,128)(2,1)S(1)}, u32[]{:S(2)}, u32[]{:S(2)}) %collective-permute-start.7) | collective-permute-done | bytes 458784 | tf_op jit(solution)/shard_map/ppermute | solution.py:287
  34.5 0.0 copy-start.6
  34.6 0.1 collective-permute-start.8
  34.7 2.5 %group.3 = (bf16[2048,768]{1,0:T(8,128)(2,1)S(1)}, f32[256,128]{1,0:T(8,128)S(1)}, s32[256,128]{1,0:T(8,128)S(1)}) custom-call(s32[33]{0:T(128)S(1)} %stack.132.src_ref, bf16[2048,768]{1,0:T(8,128)(2,1)S(1)} %get-tuple-element.16.refs_0_, f32[256,128]{1,0:T(8,128)S(1)} %get-tuple-element.17.refs_1_, ...), custom_call_target="tpu_custom_call", output_to_operand_aliasing={{0}: (1, {})} | custom-call | flops 1610612736 | tf_op jit(solution)/shard_map/group/pallas_call | solution.py:20
  37.2 0.0 collective-permute-done.8.refs_1_.refs_3_
  37.2 0.0 copy-start.4
  37.2 0.0 copy-start.5
  37.2 8.5 %score.1 = (f32[128,128]{1,0:T(8,128)}, f32[256,128]{1,0:T(8,128)S(1)}, bf16[2048,768]{1,0:T(8,128)(2,1)S(1)}) custom-call(s32[8]{0:T(128)S(1)} %copy-done.6, bf16[8,1024,768]{2,1,0:T(8,128)(2,1)S(1)} %copy-done, s32[33]{0:T(128)S(1)} %stack.132.src_ref, f32[256,128]{1,0:T(8,128)S(1)} %get-tuple-element.20.old_marks_ref, ...), custom_call_target="tpu_custom_call", output_to_operand_aliasing={{2}: (5, {})} | custom-call | tf_op jit(solution)/shard_map/score/pallas_call | solution.py:20
  45.7 5.1 %all-to-all-start = ((f32[32,4,128]{2,1,0:T(4,128)}), f32[32,4,128]{2,1,0:T(4,128)S(1)}, u32[]{:S(2)}, u32[]{:S(2)}) async-start(f32[32,4,128]{2,1,0:T(4,128)} %bitcast.33), calls=%async_computation | async-start | bytes 131072 | tf_op jit(solution)/shard_map/all_to_all | solution.py:399
  50.9 1.2 %copy-done.2 = bf16[512,896]{1,0:T(8,128)(2,1)S(1)} copy-done((bf16[512,896]{1,0:T(8,128)(2,1)S(1)}, bf16[512,896]{1,0:T(8,128)(2,1)}, u32[]{:S(2)}) %copy-start.2) | copy-done | bytes 917528
  52.1 2.5 %append.1 = (bf16[8,16,768]{2,1,0:T(8,128)(2,1)}, f32[8,16]{1,0:T(8,128)}, f32[8,768]{1,0:T(8,128)}) custom-call(s32[33]{0:T(128)S(1)} %stack.132.src_ref, f32[256,128]{1,0:T(8,128)S(1)} %get-tuple-element.20.old_marks_ref, f32[256,128]{1,0:T(8,128)S(1)} %get-tuple-element.24.marks_ref, f32[8,768]{1,0:T(8,128)S(1)} %copy-done.4, f32[8,768]{1,0:T(8,128)S(1)} %copy-done.5, ...), custom_call_target="tpu_custom_call" | custom-call | tf_op jit(solution)/shard_map/append/pallas_call | solution.py:20
  54.6 3.8 %all-to-all-done = f32[32,4,128]{2,1,0:T(4,128)S(1)} async-done(((f32[32,4,128]{2,1,0:T(4,128)}), f32[32,4,128]{2,1,0:T(4,128)S(1)}, u32[]{:S(2)}, u32[]{:S(2)}) %all-to-all-start) | async-done | bytes 65568 | tf_op jit(solution)/shard_map/all_to_all | solution.py:399
  58.4 0.9 %pick.1 = f32[16,64]{1,0:T(8,128)} custom-call(f32[128,128]{1,0:T(8,128)S(1)} %bitcast.37, s32[16,64]{1,0:T(8,128)S(1)} %bitcast.38), custom_call_target="tpu_custom_call" | custom-call | tf_op jit(solution)/shard_map/pick/pallas_call | solution.py:20
  (22 shorter events, 0.3 us)
Async XLA Ops:
  2.5 6.2 %collective-permute-start = (bf16[64,896]{1,0:T(8,128)(2,1)S(1)}, bf16[64,896]{1,0:T(8,128)(2,1)S(1)}, u32[]{:S(2)}, u32[]{:S(2)}) collective-permute-start(bf16[64,896]{1,0:T(8,128)(2,1)S(1)} %concatenate.32), channel_id=1, source_target_pairs={{0,1},{1,0},{2,3},{3,2},{4,5},{5,4},{6,7},{7,6},{8,9},{9,8},{10,11... | collective-permute-start | bytes 344072 | tf_op jit(solution)/shard_map/ppermute | solution.py:287
  5.6 11.7 %collective-permute-start.4 = (bf16[64,896]{1,0:T(8,128)(2,1)S(1)}, bf16[64,896]{1,0:T(8,128)(2,1)S(1)}, u32[]{:S(2)}, u32[]{:S(2)}) collective-permute-start(bf16[64,896]{1,0:T(8,128)(2,1)S(1)} %concatenate.32), channel_id=1, source_target_pairs={{0,2},{1,3},{2,0},{3,1},{4,6},{5,7},{6,4},{7,5},{8,10},{9,11},{10,... | collective-permute-start | bytes 344072 | tf_op jit(solution)/shard_map/ppermute | solution.py:287
  8.2 9.1 %collective-permute-start.5 = (bf16[64,896]{1,0:T(8,128)(2,1)S(1)}, bf16[64,896]{1,0:T(8,128)(2,1)S(1)}, u32[]{:S(2)}, u32[]{:S(2)}) collective-permute-start(bf16[64,896]{1,0:T(8,128)(2,1)S(1)} %concatenate.32), channel_id=1, source_target_pairs={{0,3},{1,2},{2,1},{3,0},{4,7},{5,6},{6,5},{7,4},{8,11},{9,10},{10,... | collective-permute-start | bytes 344072 | tf_op jit(solution)/shard_map/ppermute | solution.py:287
  8.8 10.1 %collective-permute-start.1 = (bf16[128,896]{1,0:T(8,128)(2,1)S(1)}, bf16[128,896]{1,0:T(8,128)(2,1)S(1)}, u32[]{:S(2)}, u32[]{:S(2)}) collective-permute-start(bf16[128,896]{1,0:T(8,128)(2,1)S(1)} %pad_maximum_fusion.3), channel_id=1, source_target_pairs={{0,8},{1,9},{2,10},{3,11},{4,20},{5,21},{6,22},{7,23},{8,0},{9,1},... | collective-permute-start | bytes 688136 | tf_op jit(solution)/shard_map/ppermute | solution.py:287
  17.3 8.6 %collective-permute-start.6 = (bf16[128,896]{1,0:T(8,128)(2,1)S(1)}, bf16[128,896]{1,0:T(8,128)(2,1)S(1)}, u32[]{:S(2)}, u32[]{:S(2)}) collective-permute-start(bf16[128,896]{1,0:T(8,128)(2,1)S(1)} %pad_maximum_fusion.4), channel_id=1, source_target_pairs={{0,8},{1,9},{2,10},{3,11},{4,20},{5,21},{6,22},{7,23},{8,0},{9,1},... | collective-permute-start | bytes 688136 | tf_op jit(solution)/shard_map/ppermute | solution.py:287
  18.9 8.7 %collective-permute-start.2 = (bf16[256,896]{1,0:T(8,128)(2,1)S(1)}, bf16[256,896]{1,0:T(8,128)(2,1)S(1)}, u32[]{:S(2)}, u32[]{:S(2)}) collective-permute-start(bf16[256,896]{1,0:T(8,128)(2,1)S(1)} %pad_maximum_fusion.1), channel_id=1, source_target_pairs={{0,16},{1,17},{2,18},{3,19},{4,12},{5,13},{6,14},{7,15},{8,24},{9,... | collective-permute-start | bytes 1376264 | tf_op jit(solution)/shard_map/ppermute | solution.py:287
  25.9 8.5 %collective-permute-start.7 = (bf16[256,896]{1,0:T(8,128)(2,1)S(1)}, bf16[256,896]{1,0:T(8,128)(2,1)S(1)}, u32[]{:S(2)}, u32[]{:S(2)}) collective-permute-start(bf16[256,896]{1,0:T(8,128)(2,1)S(1)} %pad_maximum_fusion.2), channel_id=1, source_target_pairs={{0,16},{1,17},{2,18},{3,19},{4,12},{5,13},{6,14},{7,15},{8,24},{9,... | collective-permute-start | bytes 1376264 | tf_op jit(solution)/shard_map/ppermute | solution.py:287
  27.7 9.5 %copy-start = (bf16[8,1024,768]{2,1,0:T(8,128)(2,1)S(1)}, bf16[8,1024,768]{2,1,0:T(8,128)(2,1)}, u32[]{:S(2)}) copy-start(bf16[8,1024,768]{2,1,0:T(8,128)(2,1)} %rows.1) | copy-start | bytes 37748740
  29.7 4.9 %collective-permute-start.3 = (bf16[512,896]{1,0:T(8,128)(2,1)S(1)}, bf16[512,896]{1,0:T(8,128)(2,1)S(1)}, u32[]{:S(2)}, u32[]{:S(2)}) collective-permute-start(bf16[512,896]{1,0:T(8,128)(2,1)S(1)} %pad_maximum_fusion.refs_0_), channel_id=1, source_target_pairs={{0,4},{1,5},{2,6},{3,7},{4,0},{5,1},{6,2},{7,3},{8,12},{9,13},{10,... | collective-permute-start | bytes 2752520 | tf_op jit(solution)/shard_map/ppermute | solution.py:275
  34.5 2.7 %copy-start.6 = (s32[8]{0:T(128)S(1)}, s32[8]{0:T(128)}, u32[]{:S(2)}) copy-start(s32[8]{0:T(128)} %fill_ref.1) | copy-start | bytes 100
  34.6 2.6 %collective-permute-start.8 = (bf16[512,896]{1,0:T(8,128)(2,1)S(1)}, bf16[512,896]{1,0:T(8,128)(2,1)S(1)}, u32[]{:S(2)}, u32[]{:S(2)}) collective-permute-start(bf16[512,896]{1,0:T(8,128)(2,1)S(1)} %constant_dynamic-update-slice_fusion.refs_0_.refs_2_), channel_id=1, source_target_pairs={{0,4},{1,5},{2,6},{3,7},{4,0},{5,1},{6,2},{7,3},{8,12},{9,13},{10,... | collective-permute-start | bytes 2752520 | tf_op jit(solution)/shard_map/ppermute | solution.py:275
  34.6 2.5 %copy-start.1 = (bf16[512,896]{1,0:T(8,128)(2,1)}, bf16[512,896]{1,0:T(8,128)(2,1)S(1)}, u32[]{:S(2)}) copy-start(bf16[512,896]{1,0:T(8,128)(2,1)S(1)} %collective-permute-done.3.refs_3_.refs_1_) | copy-start | bytes 2752516
  37.2 13.7 %copy-start.4 = (f32[8,768]{1,0:T(8,128)S(1)}, f32[8,768]{1,0:T(8,128)}, u32[]{:S(2)}) copy-start(f32[8,768]{1,0:T(8,128)} %center_ref.1) | copy-start | bytes 73732
  37.2 13.7 %copy-start.5 = (f32[8,768]{1,0:T(8,128)S(1)}, f32[8,768]{1,0:T(8,128)}, u32[]{:S(2)}) copy-start(f32[8,768]{1,0:T(8,128)} %sums_ref.1) | copy-start | bytes 73732
  45.7 12.6 %all-to-all-start = ((f32[32,4,128]{2,1,0:T(4,128)}), f32[32,4,128]{2,1,0:T(4,128)S(1)}, u32[]{:S(2)}, u32[]{:S(2)}) async-start(f32[32,4,128]{2,1,0:T(4,128)} %bitcast.33), calls=%async_computation | async-start | bytes 131072 | tf_op jit(solution)/shard_map/all_to_all | solution.py:399
  50.9 1.2 %copy-start.2 = (bf16[512,896]{1,0:T(8,128)(2,1)S(1)}, bf16[512,896]{1,0:T(8,128)(2,1)}, u32[]{:S(2)}) copy-start(bf16[512,896]{1,0:T(8,128)(2,1)} %copy-done.1) | copy-start | bytes 2752516
  52.1 6.3 %copy-start.3 = (s32[64,16]{0,1:T(8,128)S(1)}, s32[64,16]{0,1:T(8,128)}, u32[]{:S(2)}) copy-start(s32[64,16]{0,1:T(8,128)} %param.8) | copy-start | bytes 12292
where the time goes:
time: 59.5 us; the launch traced here: 59.3 us
  waiting for transfers between devices  19.9 us (33%)
  starting transfers between devices  18.6 us (31%)
  Pallas kernels  16.5 us (28%)
  local copies, waits for them, and re-layouts  2.51 us (4%)
  other arithmetic  0.95 us (2%)
  between operations  0.84 us (1%)
    pallas_call x5, Pallas kernels, call(): pl.pallas_call(body, in_specs=list(specs), out_specs=[VMEM] * len(out_sha...  16.5 us
    ppermute x7, waiting for transfers between devices, send(): return lax.ppermute(x, AXES, swap_pairs(rows, cols, of))  16.1 us
    ppermute x7, starting transfers between devices, send(): return lax.ppermute(x, AXES, swap_pairs(rows, cols, of))  13.4 us
    all_to_all x1, starting transfers between devices, local(): lax.all_to_all(best.reshape(group, list_count // 2, width), AXES, split_a...  5.14 us
    all_to_all x1, waiting for transfers between devices, local(): lax.all_to_all(best.reshape(group, list_count // 2, width), AXES, split_a...  3.8 us
    unnamed x17, local copies, waits for them, and re-layouts  1.26 us
  transfers between devices with their start and end apart: 10, of which 5 were waited for; matrix products, arithmetic and copies ran while one was open for 1% of the time, Pallas kernels for 12%

commit v1 on v0

--- a/solution.py
+++ b/solution.py
@@ -12,7 +12,7 @@
 SMEM = pl.BlockSpec(memory_space=pltpu.SMEM)
 BF16 = jnp.bfloat16
 F32 = jnp.float32
-LISTS_A_STEP = 4
+LISTS_A_STEP = 8
 
 
 def call(body, out_shape, *args, specs, name, scratch=(), flops=0, limit=24, alias=None):

time: 59.5 us -> 59.4 us (level)
  no operation moved by 1% of the time
where the time goes in v1:
time: 59.4 us; the launch traced here: 59.2 us
  waiting for transfers between devices  19.9 us (34%)
  starting transfers between devices  18.6 us (31%)
  Pallas kernels  16.3 us (27%)
  local copies, waits for them, and re-layouts  2.51 us (4%)
  other arithmetic  0.95 us (2%)
  between operations  0.84 us (1%)
    pallas_call x5, Pallas kernels, call(): pl.pallas_call(body, in_specs=list(specs), out_specs=[VMEM] * len(out_sha...  16.3 us
    ppermute x7, waiting for transfers between devices, send(): return lax.ppermute(x, AXES, swap_pairs(rows, cols, of))  16.1 us
    ppermute x7, starting transfers between devices, send(): return lax.ppermute(x, AXES, swap_pairs(rows, cols, of))  13.4 us
    all_to_all x1, starting transfers between devices, local(): lax.all_to_all(best.reshape(group, list_count // 2, width), AXES, split_a...  5.13 us
    all_to_all x1, waiting for transfers between devices, local(): lax.all_to_all(best.reshape(group, list_count // 2, width), AXES, split_a...  3.79 us
    unnamed x17, local copies, waits for them, and re-layouts  1.26 us
  transfers between devices with their start and end apart: 10, of which 5 were waited for; matrix products, arithmetic and copies ran while one was open for 1% of the time, Pallas kernels for 12%

profile of v1, /device:TPU:0, one launch (start us, length us, event | category | flops | bytes accessed | tf_op | source)
XLA Modules:
  0.0 59.2 jit_solution(17720504809331727010)
XLA Ops:
  0.6 0.7 %pad_add_fusion = s32[64,17]{0,1:T(8,128)S(1)} fusion(s32[64,1]{0,1:T(1,128)} %bitcast.40, s32[64,16]{0,1:T(8,128)} %param.8), kind=kLoop, calls=%fused_computation.15 | loop fusion | flops 1088 | bytes 8704 | tf_op jit(solution)/shard_map/concatenate | solution.py:336
  1.4 0.1 copy.15
  1.5 1.0 %concatenate.32 = bf16[64,896]{1,0:T(8,128)(2,1)S(1)} concatenate(bf16[64,768]{1,0:T(8,128)(2,1)} %param.7, bf16[64,17]{1,0:T(8,128)(2,1)S(1)} %get-tuple-element.29, bf16[64,47]{1,0:T(8,128)(2,1)S(1)} %broadcast_in_dim.7, bf16[64,17]{1,0:T(8,128)(2,1)S(1)} %get-tuple-element.28, bf16[64,47]{1,0:T(8,128)(2,1)S(1)} %broadcast_in_dim.7), dimensions={1} | concatenate | bytes 229376 | tf_op jit(solution)/shard_map/concatenate | solution.py:341
  2.5 3.1 %collective-permute-start = (bf16[64,896]{1,0:T(8,128)(2,1)S(1)}, bf16[64,896]{1,0:T(8,128)(2,1)S(1)}, u32[]{:S(2)}, u32[]{:S(2)}) collective-permute-start(bf16[64,896]{1,0:T(8,128)(2,1)S(1)} %concatenate.32), channel_id=1, source_target_pairs={{0,1},{1,0},{2,3},{3,2},{4,5},{5,4},{6,7},{7,6},{8,9},{9,8},{10,11... | collective-permute-start | bytes 344072 | tf_op jit(solution)/shard_map/ppermute | solution.py:287
  5.6 2.6 %collective-permute-start.4 = (bf16[64,896]{1,0:T(8,128)(2,1)S(1)}, bf16[64,896]{1,0:T(8,128)(2,1)S(1)}, u32[]{:S(2)}, u32[]{:S(2)}) collective-permute-start(bf16[64,896]{1,0:T(8,128)(2,1)S(1)} %concatenate.32), channel_id=1, source_target_pairs={{0,2},{1,3},{2,0},{3,1},{4,6},{5,7},{6,4},{7,5},{8,10},{9,11},{10,... | collective-permute-start | bytes 344072 | tf_op jit(solution)/shard_map/ppermute | solution.py:287
  8.2 0.6 collective-permute-done
  8.8 2.9 %collective-permute-start.1 = (bf16[128,896]{1,0:T(8,128)(2,1)S(1)}, bf16[128,896]{1,0:T(8,128)(2,1)S(1)}, u32[]{:S(2)}, u32[]{:S(2)}) collective-permute-start(bf16[128,896]{1,0:T(8,128)(2,1)S(1)} %pad_maximum_fusion.3), channel_id=1, source_target_pairs={{0,8},{1,9},{2,10},{3,11},{4,20},{5,21},{6,22},{7,23},{8,0},{9,1},... | collective-permute-start | bytes 688136 | tf_op jit(solution)/shard_map/ppermute | solution.py:287
  11.7 5.6 %collective-permute-done.4 = bf16[64,896]{1,0:T(8,128)(2,1)S(1)} collective-permute-done((bf16[64,896]{1,0:T(8,128)(2,1)S(1)}, bf16[64,896]{1,0:T(8,128)(2,1)S(1)}, u32[]{:S(2)}, u32[]{:S(2)}) %collective-permute-start.4) | collective-permute-done | bytes 114720 | tf_op jit(solution)/shard_map/ppermute | solution.py:287
  17.3 1.6 %collective-permute-start.6 = (bf16[128,896]{1,0:T(8,128)(2,1)S(1)}, bf16[128,896]{1,0:T(8,128)(2,1)S(1)}, u32[]{:S(2)}, u32[]{:S(2)}) collective-permute-start(bf16[128,896]{1,0:T(8,128)(2,1)S(1)} %pad_maximum_fusion.4), channel_id=1, source_target_pairs={{0,8},{1,9},{2,10},{3,11},{4,20},{5,21},{6,22},{7,23},{8,0},{9,1},... | collective-permute-start | bytes 688136 | tf_op jit(solution)/shard_map/ppermute | solution.py:287
  18.9 0.0 collective-permute-done.1
  18.9 1.6 %collective-permute-start.2 = (bf16[256,896]{1,0:T(8,128)(2,1)S(1)}, bf16[256,896]{1,0:T(8,128)(2,1)S(1)}, u32[]{:S(2)}, u32[]{:S(2)}) collective-permute-start(bf16[256,896]{1,0:T(8,128)(2,1)S(1)} %pad_maximum_fusion.1), channel_id=1, source_target_pairs={{0,16},{1,17},{2,18},{3,19},{4,12},{5,13},{6,14},{7,15},{8,24},{9,... | collective-permute-start | bytes 1376264 | tf_op jit(solution)/shard_map/ppermute | solution.py:287
  20.5 0.1 stack.132.src_ref
  20.6 5.3 %collective-permute-done.6 = bf16[128,896]{1,0:T(8,128)(2,1)S(1)} collective-permute-done((bf16[128,896]{1,0:T(8,128)(2,1)S(1)}, bf16[128,896]{1,0:T(8,128)(2,1)S(1)}, u32[]{:S(2)}, u32[]{:S(2)}) %collective-permute-start.6) | collective-permute-done | bytes 229408 | tf_op jit(solution)/shard_map/ppermute | solution.py:287
  25.9 1.6 %collective-permute-start.7 = (bf16[256,896]{1,0:T(8,128)(2,1)S(1)}, bf16[256,896]{1,0:T(8,128)(2,1)S(1)}, u32[]{:S(2)}, u32[]{:S(2)}) collective-permute-start(bf16[256,896]{1,0:T(8,128)(2,1)S(1)} %pad_maximum_fusion.2), channel_id=1, source_target_pairs={{0,16},{1,17},{2,18},{3,19},{4,12},{5,13},{6,14},{7,15},{8,24},{9,... | collective-permute-start | bytes 1376264 | tf_op jit(solution)/shard_map/ppermute | solution.py:287
  27.6 0.0 collective-permute-done.2
  27.6 0.1 pad_maximum_fusion.refs_0_
  27.7 0.0 copy-start
  27.7 2.0 %group.2 = (bf16[2048,768]{1,0:T(8,128)(2,1)S(1)}, f32[256,128]{1,0:T(8,128)S(1)}, s32[256,128]{1,0:T(8,128)S(1)}) custom-call(s32[33]{0:T(128)S(1)} %stack.132.src_ref, bf16[512,896]{1,0:T(8,128)(2,1)S(1)} %pad_maximum_fusion.refs_0_), custom_call_target="tpu_custom_call" | custom-call | flops 1610612736 | tf_op jit(solution)/shard_map/group/pallas_call | solution.py:20
  29.7 0.1 collective-permute-start.3
  29.8 4.7 %collective-permute-done.7 = bf16[256,896]{1,0:T(8,128)(2,1)S(1)} collective-permute-done((bf16[256,896]{1,0:T(8,128)(2,1)S(1)}, bf16[256,896]{1,0:T(8,128)(2,1)S(1)}, u32[]{:S(2)}, u32[]{:S(2)}) %collective-permute-start.7) | collective-permute-done | bytes 458784 | tf_op jit(solution)/shard_map/ppermute | solution.py:287
  34.5 0.0 copy-start.6
  34.6 0.1 collective-permute-start.8
  34.7 2.5 %group.3 = (bf16[2048,768]{1,0:T(8,128)(2,1)S(1)}, f32[256,128]{1,0:T(8,128)S(1)}, s32[256,128]{1,0:T(8,128)S(1)}) custom-call(s32[33]{0:T(128)S(1)} %stack.132.src_ref, bf16[2048,768]{1,0:T(8,128)(2,1)S(1)} %get-tuple-element.16.refs_0_, f32[256,128]{1,0:T(8,128)S(1)} %get-tuple-element.17.refs_1_, ...), custom_call_target="tpu_custom_call", output_to_operand_aliasing={{0}: (1, {})} | custom-call | flops 1610612736 | tf_op jit(solution)/shard_map/group/pallas_call | solution.py:20
  37.1 0.0 collective-permute-done.8.refs_1_.refs_3_
  37.2 0.0 copy-start.4
  37.2 0.0 copy-start.5
  37.2 8.5 %score.1 = (f32[128,128]{1,0:T(8,128)}, f32[256,128]{1,0:T(8,128)S(1)}, bf16[2048,768]{1,0:T(8,128)(2,1)S(1)}) custom-call(s32[8]{0:T(128)S(1)} %copy-done.6, bf16[8,1024,768]{2,1,0:T(8,128)(2,1)S(1)} %copy-done, s32[33]{0:T(128)S(1)} %stack.132.src_ref, f32[256,128]{1,0:T(8,128)S(1)} %get-tuple-element.20.old_marks_ref, ...), custom_call_target="tpu_custom_call", output_to_operand_aliasing={{2}: (5, {})} | custom-call | tf_op jit(solution)/shard_map/score/pallas_call | solution.py:20
  45.6 5.1 %all-to-all-start = ((f32[32,4,128]{2,1,0:T(4,128)}), f32[32,4,128]{2,1,0:T(4,128)S(1)}, u32[]{:S(2)}, u32[]{:S(2)}) async-start(f32[32,4,128]{2,1,0:T(4,128)} %bitcast.33), calls=%async_computation | async-start | bytes 131072 | tf_op jit(solution)/shard_map/all_to_all | solution.py:399
  50.8 1.2 %copy-done.2 = bf16[512,896]{1,0:T(8,128)(2,1)S(1)} copy-done((bf16[512,896]{1,0:T(8,128)(2,1)S(1)}, bf16[512,896]{1,0:T(8,128)(2,1)}, u32[]{:S(2)}) %copy-start.2) | copy-done | bytes 917528
  52.0 2.5 %append.1 = (bf16[8,16,768]{2,1,0:T(8,128)(2,1)}, f32[8,16]{1,0:T(8,128)}, f32[8,768]{1,0:T(8,128)}) custom-call(s32[33]{0:T(128)S(1)} %stack.132.src_ref, f32[256,128]{1,0:T(8,128)S(1)} %get-tuple-element.20.old_marks_ref, f32[256,128]{1,0:T(8,128)S(1)} %get-tuple-element.24.marks_ref, f32[8,768]{1,0:T(8,128)S(1)} %copy-done.4, f32[8,768]{1,0:T(8,128)S(1)} %copy-done.5, ...), custom_call_target="tpu_custom_call" | custom-call | tf_op jit(solution)/shard_map/append/pallas_call | solution.py:20
  54.5 3.8 %all-to-all-done = f32[32,4,128]{2,1,0:T(4,128)S(1)} async-done(((f32[32,4,128]{2,1,0:T(4,128)}), f32[32,4,128]{2,1,0:T(4,128)S(1)}, u32[]{:S(2)}, u32[]{:S(2)}) %all-to-all-start) | async-done | bytes 65568 | tf_op jit(solution)/shard_map/all_to_all | solution.py:399
  58.3 0.9 %pick.1 = f32[16,64]{1,0:T(8,128)} custom-call(f32[128,128]{1,0:T(8,128)S(1)} %bitcast.37, s32[16,64]{1,0:T(8,128)S(1)} %bitcast.38), custom_call_target="tpu_custom_call" | custom-call | tf_op jit(solution)/shard_map/pick/pallas_call | solution.py:20
  (22 shorter events, 0.3 us)
Async XLA Ops:
  2.5 6.2 %collective-permute-start = (bf16[64,896]{1,0:T(8,128)(2,1)S(1)}, bf16[64,896]{1,0:T(8,128)(2,1)S(1)}, u32[]{:S(2)}, u32[]{:S(2)}) collective-permute-start(bf16[64,896]{1,0:T(8,128)(2,1)S(1)} %concatenate.32), channel_id=1, source_target_pairs={{0,1},{1,0},{2,3},{3,2},{4,5},{5,4},{6,7},{7,6},{8,9},{9,8},{10,11... | collective-permute-start | bytes 344072 | tf_op jit(solution)/shard_map/ppermute | solution.py:287
  5.6 11.7 %collective-permute-start.4 = (bf16[64,896]{1,0:T(8,128)(2,1)S(1)}, bf16[64,896]{1,0:T(8,128)(2,1)S(1)}, u32[]{:S(2)}, u32[]{:S(2)}) collective-permute-start(bf16[64,896]{1,0:T(8,128)(2,1)S(1)} %concatenate.32), channel_id=1, source_target_pairs={{0,2},{1,3},{2,0},{3,1},{4,6},{5,7},{6,4},{7,5},{8,10},{9,11},{10,... | collective-permute-start | bytes 344072 | tf_op jit(solution)/shard_map/ppermute | solution.py:287
  8.2 9.1 %collective-permute-start.5 = (bf16[64,896]{1,0:T(8,128)(2,1)S(1)}, bf16[64,896]{1,0:T(8,128)(2,1)S(1)}, u32[]{:S(2)}, u32[]{:S(2)}) collective-permute-start(bf16[64,896]{1,0:T(8,128)(2,1)S(1)} %concatenate.32), channel_id=1, source_target_pairs={{0,3},{1,2},{2,1},{3,0},{4,7},{5,6},{6,5},{7,4},{8,11},{9,10},{10,... | collective-permute-start | bytes 344072 | tf_op jit(solution)/shard_map/ppermute | solution.py:287
  8.8 10.1 %collective-permute-start.1 = (bf16[128,896]{1,0:T(8,128)(2,1)S(1)}, bf16[128,896]{1,0:T(8,128)(2,1)S(1)}, u32[]{:S(2)}, u32[]{:S(2)}) collective-permute-start(bf16[128,896]{1,0:T(8,128)(2,1)S(1)} %pad_maximum_fusion.3), channel_id=1, source_target_pairs={{0,8},{1,9},{2,10},{3,11},{4,20},{5,21},{6,22},{7,23},{8,0},{9,1},... | collective-permute-start | bytes 688136 | tf_op jit(solution)/shard_map/ppermute | solution.py:287
  17.3 8.6 %collective-permute-start.6 = (bf16[128,896]{1,0:T(8,128)(2,1)S(1)}, bf16[128,896]{1,0:T(8,128)(2,1)S(1)}, u32[]{:S(2)}, u32[]{:S(2)}) collective-permute-start(bf16[128,896]{1,0:T(8,128)(2,1)S(1)} %pad_maximum_fusion.4), channel_id=1, source_target_pairs={{0,8},{1,9},{2,10},{3,11},{4,20},{5,21},{6,22},{7,23},{8,0},{9,1},... | collective-permute-start | bytes 688136 | tf_op jit(solution)/shard_map/ppermute | solution.py:287
  18.9 8.7 %collective-permute-start.2 = (bf16[256,896]{1,0:T(8,128)(2,1)S(1)}, bf16[256,896]{1,0:T(8,128)(2,1)S(1)}, u32[]{:S(2)}, u32[]{:S(2)}) collective-permute-start(bf16[256,896]{1,0:T(8,128)(2,1)S(1)} %pad_maximum_fusion.1), channel_id=1, source_target_pairs={{0,16},{1,17},{2,18},{3,19},{4,12},{5,13},{6,14},{7,15},{8,24},{9,... | collective-permute-start | bytes 1376264 | tf_op jit(solution)/shard_map/ppermute | solution.py:287
  25.9 8.5 %collective-permute-start.7 = (bf16[256,896]{1,0:T(8,128)(2,1)S(1)}, bf16[256,896]{1,0:T(8,128)(2,1)S(1)}, u32[]{:S(2)}, u32[]{:S(2)}) collective-permute-start(bf16[256,896]{1,0:T(8,128)(2,1)S(1)} %pad_maximum_fusion.2), channel_id=1, source_target_pairs={{0,16},{1,17},{2,18},{3,19},{4,12},{5,13},{6,14},{7,15},{8,24},{9,... | collective-permute-start | bytes 1376264 | tf_op jit(solution)/shard_map/ppermute | solution.py:287
  27.7 9.5 %copy-start = (bf16[8,1024,768]{2,1,0:T(8,128)(2,1)S(1)}, bf16[8,1024,768]{2,1,0:T(8,128)(2,1)}, u32[]{:S(2)}) copy-start(bf16[8,1024,768]{2,1,0:T(8,128)(2,1)} %rows.1) | copy-start | bytes 37748740
  29.7 4.9 %collective-permute-start.3 = (bf16[512,896]{1,0:T(8,128)(2,1)S(1)}, bf16[512,896]{1,0:T(8,128)(2,1)S(1)}, u32[]{:S(2)}, u32[]{:S(2)}) collective-permute-start(bf16[512,896]{1,0:T(8,128)(2,1)S(1)} %pad_maximum_fusion.refs_0_), channel_id=1, source_target_pairs={{0,4},{1,5},{2,6},{3,7},{4,0},{5,1},{6,2},{7,3},{8,12},{9,13},{10,... | collective-permute-start | bytes 2752520 | tf_op jit(solution)/shard_map/ppermute | solution.py:275
  34.5 2.6 %copy-start.6 = (s32[8]{0:T(128)S(1)}, s32[8]{0:T(128)}, u32[]{:S(2)}) copy-start(s32[8]{0:T(128)} %fill_ref.1) | copy-start | bytes 100
  34.6 2.6 %collective-permute-start.8 = (bf16[512,896]{1,0:T(8,128)(2,1)S(1)}, bf16[512,896]{1,0:T(8,128)(2,1)S(1)}, u32[]{:S(2)}, u32[]{:S(2)}) collective-permute-start(bf16[512,896]{1,0:T(8,128)(2,1)S(1)} %constant_dynamic-update-slice_fusion.refs_0_.refs_2_), channel_id=1, source_target_pairs={{0,4},{1,5},{2,6},{3,7},{4,0},{5,1},{6,2},{7,3},{8,12},{9,13},{10,... | collective-permute-start | bytes 2752520 | tf_op jit(solution)/shard_map/ppermute | solution.py:275
  34.6 2.5 %copy-start.1 = (bf16[512,896]{1,0:T(8,128)(2,1)}, bf16[512,896]{1,0:T(8,128)(2,1)S(1)}, u32[]{:S(2)}) copy-start(bf16[512,896]{1,0:T(8,128)(2,1)S(1)} %collective-permute-done.3.refs_3_.refs_1_) | copy-start | bytes 2752516
  37.2 13.6 %copy-start.4 = (f32[8,768]{1,0:T(8,128)S(1)}, f32[8,768]{1,0:T(8,128)}, u32[]{:S(2)}) copy-start(f32[8,768]{1,0:T(8,128)} %center_ref.1) | copy-start | bytes 73732
  37.2 13.6 %copy-start.5 = (f32[8,768]{1,0:T(8,128)S(1)}, f32[8,768]{1,0:T(8,128)}, u32[]{:S(2)}) copy-start(f32[8,768]{1,0:T(8,128)} %sums_ref.1) | copy-start | bytes 73732
  45.6 12.6 %all-to-all-start = ((f32[32,4,128]{2,1,0:T(4,128)}), f32[32,4,128]{2,1,0:T(4,128)S(1)}, u32[]{:S(2)}, u32[]{:S(2)}) async-start(f32[32,4,128]{2,1,0:T(4,128)} %bitcast.33), calls=%async_computation | async-start | bytes 131072 | tf_op jit(solution)/shard_map/all_to_all | solution.py:399
  50.8 1.2 %copy-start.2 = (bf16[512,896]{1,0:T(8,128)(2,1)S(1)}, bf16[512,896]{1,0:T(8,128)(2,1)}, u32[]{:S(2)}) copy-start(bf16[512,896]{1,0:T(8,128)(2,1)} %copy-done.1) | copy-start | bytes 2752516
  52.0 6.3 %copy-start.3 = (s32[64,16]{0,1:T(8,128)S(1)}, s32[64,16]{0,1:T(8,128)}, u32[]{:S(2)}) copy-start(s32[64,16]{0,1:T(8,128)} %param.8) | copy-start | bytes 12292
